TPU v7x, 32 devices: a whole 2x2x4 slice. The times are simulated.
32 devices in a mesh: group: 2 (over y), node: 8 (over z, x), tp: 2 (over core).
Axes of the slice: x: 2, y: 2, z: 4, core: 2. Of those that a mesh axis runs over, the one named last changes fastest.
Arguments:
- residual: bfloat16 [256, 6144], P(('group', 'node'), 'tp'), parts along dimension 0, may hold values from -70 to 70
- queries: bfloat16 [256, 6144], P(('group', 'node'), 'tp'), parts along dimension 0, may hold values from -150 to 150
- new_keys: bfloat16 [256, 1024], P(('group', 'node'), 'tp'), parts along dimension 0, may hold values from -5 to 5
- new_values: bfloat16 [256, 1024], P(('group', 'node'), 'tp'), parts along dimension 0, may hold values from -6 to 6
- cache_keys: bfloat16 [256, 8, 96, 128], P(('group', 'node'), 'tp'), parts along dimension 0, may hold values from -5 to 5
- cache_values: bfloat16 [256, 8, 96, 128], P(('group', 'node'), 'tp'), parts along dimension 0, may hold values from -6 to 6
- lengths: int32 [256], P(('group', 'node')), parts along dimension 0, may hold values from 1 to 96, as said below
- routes: int32 [256, 2], P(('group', 'node')), parts along dimension 0, may hold values from 0 to 3, all different within a row; in each aligned block of 16 rows (0 to 15, 16 to 31, ...) at most 9 rows name the same one
- norm_gain: float32 [6144], P('tp'), may hold values from 0.1 to 1.9
- router_weight: bfloat16 [6144, 4], P('tp'), may hold values from -0.078125 to 0.078125
- gate_weight: bfloat16 [6144, 32768], P('tp', 'node'), may hold values from -0.078125 to 0.078125
- up_weight: bfloat16 [6144, 32768], P('tp', 'node'), may hold values from -0.078125 to 0.078125
- down_weight: bfloat16 [32768, 6144], P('node', 'tp'), may hold values from -0.0625 to 0.0625
Outputs:
- mixed: bfloat16 [256, 6144], P(('group', 'node'), 'tp'), parts along dimension 0
There are 2 independent parts, one for each index of `group`. A program takes and returns all parts, laid end to end along the dimension named above; an argument that names none is the same for every part. Nothing has to cross between parts.
Inputs may be any that keep to these rules, and one draw needn't show every extreme that they name: `routes`: each row names two different experts; within each aligned block of 16 rows (the rows of one node index) no expert is named by more than 9 rows. `lengths`: some row's cache is full.
All inputs are finite; a program needn't handle non-finite values.
Results may differ from a plain program's by a relative error of at most 0.005.
Values may be sent and summed in bfloat16 or wider, within the bound.
A program may use at most 192 MiB of HBM per device.

v0:
```python
import math

import jax
import jax.numpy as jnp
from jax import lax
from jax.sharding import PartitionSpec as P


def attention_rows(queries, new_keys, new_values, cache_keys, cache_values, lengths):
    row_count, kv_local, cache_len, head_dim = cache_keys.shape
    query_grid = queries.reshape(row_count, kv_local, -1, head_dim)
    factor = 1.0 / math.sqrt(head_dim)
    scores = (
        jnp.einsum("rkgd,rkld->rkgl", query_grid, cache_keys, preferred_element_type=jnp.float32)
        * factor
    )
    position = lax.broadcasted_iota(jnp.int32, (1, 1, 1, cache_len), 3)
    scores = jnp.where(position < lengths[:, None, None, None], scores, -jnp.inf)
    own_key = new_keys.reshape(row_count, kv_local, head_dim)
    own_score = (
        jnp.einsum("rkgd,rkd->rkg", query_grid, own_key, preferred_element_type=jnp.float32)
        * factor
    )
    highest = jnp.maximum(jnp.max(scores, axis=3), own_score)
    weights = jnp.exp(scores - highest[..., None])
    own_weight = jnp.exp(own_score - highest)
    denominator = jnp.sum(weights, axis=3) + own_weight
    attn_probs = (weights / denominator[..., None]).astype(jnp.bfloat16)
    own_prob = (own_weight / denominator).astype(jnp.bfloat16)
    attended = jnp.einsum(
        "rkgl,rkld->rkgd", attn_probs, cache_values, preferred_element_type=jnp.float32
    )
    own_value = new_values.reshape(row_count, kv_local, 1, head_dim).astype(jnp.float32)
    attended = attended + own_prob.astype(jnp.float32)[..., None] * own_value
    return attended.reshape(row_count, -1)


def expert_block(incoming, gate_weight, up_weight, down_weight):
    sources, slot_part, half_width = incoming.shape
    flattened = incoming.reshape(sources * slot_part, half_width)
    gate_part = jnp.dot(flattened, gate_weight, preferred_element_type=jnp.float32)
    up_part = jnp.dot(flattened, up_weight, preferred_element_type=jnp.float32)
    gate_value, up_value = lax.psum((gate_part, up_part), "tp")
    hidden = (jax.nn.silu(gate_value) * up_value).astype(jnp.bfloat16)
    produced = jnp.dot(hidden, down_weight, preferred_element_type=jnp.float32).astype(jnp.bfloat16)
    return produced.reshape(sources, slot_part, -1)


def local(
    residual,
    queries,
    new_keys,
    new_values,
    cache_keys,
    cache_values,
    lengths,
    routes,
    norm_gain,
    router_weight,
    gate_weight,
    up_weight,
    down_weight,
):
    row_count, half_width = residual.shape
    full_width = half_width * lax.axis_size("tp")
    expert_count = router_weight.shape[1]
    node_count = lax.axis_size("node")
    per_expert = node_count // expert_count
    slot_count = row_count // 2 + 1
    mixed_in = residual.astype(jnp.float32) + attention_rows(
        queries, new_keys, new_values, cache_keys, cache_values, lengths
    )
    square_sum = lax.psum(jnp.sum(mixed_in * mixed_in, axis=1), "tp")
    inverse = lax.rsqrt(square_sum / full_width + 1e-05)
    normed = (mixed_in * inverse[:, None] * norm_gain).astype(jnp.bfloat16)
    logits = lax.psum(jnp.dot(normed, router_weight, preferred_element_type=jnp.float32), "tp")
    expert_ids = lax.broadcasted_iota(jnp.int32, (1, expert_count), 1)
    slot_ids = lax.broadcasted_iota(jnp.int32, (1, slot_count, 1), 1)
    flat_routes = routes.reshape(-1)
    onehot = (flat_routes[:, None] == expert_ids).astype(jnp.int32)
    earlier = jnp.cumsum(onehot, axis=0) - onehot
    slot_of = jnp.sum(earlier * onehot, axis=1)
    chosen = onehot.reshape(row_count, 2, expert_count).astype(jnp.float32)
    picked = jnp.sum(chosen * logits[:, None, :], axis=2)
    first_weight = jax.nn.sigmoid(picked[:, 0] - picked[:, 1])
    second_weight = jax.nn.sigmoid(picked[:, 1] - picked[:, 0])
    pair_weight = jnp.stack([first_weight, second_weight], axis=1)
    slot_match = (
        slot_of.reshape(row_count, 2)[:, :, None] == slot_ids[0, :, 0][None, None, :]
    ).astype(jnp.float32)
    combine = jnp.einsum(
        "rk,rke,rks->res", pair_weight, chosen, slot_match, precision=lax.Precision.HIGHEST
    )
    selector = onehot.T[:, None, :] * (slot_of[None, None, :] == slot_ids).astype(jnp.int32)
    selector = jnp.sum(selector.reshape(expert_count, slot_count, row_count, 2), axis=3).astype(
        jnp.bfloat16
    )
    outgoing = jnp.einsum(
        "esr,rd->esd", selector, normed, preferred_element_type=jnp.float32
    ).astype(jnp.bfloat16)
    outgoing = jnp.repeat(outgoing, per_expert, axis=0)
    computed = expert_block(
        lax.all_to_all(outgoing, "node", split_axis=0, concat_axis=0, tiled=True),
        gate_weight,
        up_weight,
        down_weight,
    )
    returned = lax.all_to_all(computed, "node", split_axis=0, concat_axis=0, tiled=True)
    summed = jnp.sum(
        returned.astype(jnp.float32).reshape(expert_count, per_expert, slot_count, half_width),
        axis=1,
    )
    expert_sum = jnp.einsum("res,esd->rd", combine, summed, precision=lax.Precision.HIGHEST)
    return (mixed_in + expert_sum).astype(jnp.bfloat16)


def solution(mesh):
    placed = (
        P(("group", "node"), "tp"),
        P(("group", "node"), "tp"),
        P(("group", "node"), "tp"),
        P(("group", "node"), "tp"),
        P(("group", "node"), "tp", None, None),
        P(("group", "node"), "tp", None, None),
        P(("group", "node")),
        P(("group", "node"), None),
        P("tp"),
        P("tp", None),
        P("tp", "node"),
        P("tp", "node"),
        P("node", "tp"),
    )
    return jax.shard_map(
        local, mesh=mesh, in_specs=placed, out_specs=P(("group", "node"), "tp"), check_vma=False
    )
```

profile of v0, /device:TPU:0, one launch (start us, length us, event | category | flops | bytes accessed | tf_op | source)
XLA Modules:
  0.0 139.9 jit_solution(17723896120616151397)
XLA Ops:
  6.5 0.8 fusion.22
  7.3 0.8 copy.42
  8.1 0.7 iota_compare_fusion.1
  9.0 0.2 select_reduce_fusion
  9.3 0.1 copy.48
  9.5 0.7 reshape.142
  10.2 0.7 reshape.134
  10.9 1.0 reshape.126
  12.0 0.2 fusion.26
  12.2 2.4 %fusion.25 = (f32[16,4,6]{2,1,0:T(4,128)S(1)}, f32[16,4,6,96]{3,2,1,0:T(8,128)S(1)}) fusion(bf16[16,4,6,128]{3,2,1,0:T(8,128)(2,1)S(1)} %reshape.126, bf16[16,4,96,128]{3,2,1,0:T(8,128)(2,1)} %param.17, pred[16,96]{1,0:T(8,128)(4,1)S(1)} %iota_compare_fusion.1), kind=kOutput, calls=%fused_computation.51 | convolution fusion | flops 9547392 | bytes 1821696 | tf_op jit(solution)/shard_map/rkgd,rkld->rkgl/dot_general | solution.py:14
  14.6 0.3 fusion.4
  15.0 0.6 convolution_add_fusion
  15.6 0.2 copy-done.2
  15.9 0.1 multiply_reduce_fusion
  16.0 2.6 %psum.28 = f32[16]{0:T(128)S(1)} all-reduce(f32[16]{0:T(128)S(1)} %multiply_reduce_fusion), channel_id=1, replica_groups=mesh['group'=2,'node'=8,'tp'=2] {'tp'}, use_global_device_ids=true, to_apply=%region_3.4 | all-reduce | flops 16 | bytes 128 | tf_op jit(solution)/shard_map/psum | solution.py:73
  18.7 0.2 convolution_convert_fusion.1
  19.0 27.4 %all_to_all.10 = bf16[8,9,3072]{2,1,0:T(8,128)(2,1)S(1)} all-to-all(bf16[8,9,3072]{2,1,0:T(8,128)(2,1)S(1)} %bitcast.28), channel_id=1, replica_groups=mesh['group'=2,'node'=8,'tp'=2] {'node'}, dimensions={0} | all-to-all | bytes 884736 | tf_op jit(solution)/shard_map/all_to_all | solution.py:103
  46.4 0.2 reshape.130
  46.6 11.5 %fusion.29 = f32[72,4096]{1,0:T(8,128)} fusion(bf16[72,3072]{1,0:T(8,128)(2,1)S(1)} %reshape.130, bf16[3072,4096]{1,0:T(8,128)(2,1)} %param.24), kind=kOutput, calls=%fused_computation.55 | convolution fusion | flops 1811939328 | bytes 26787840 | tf_op jit(solution)/shard_map/dot_general | solution.py:42
  58.1 11.5 %fusion.28 = f32[72,4096]{1,0:T(8,128)} fusion(bf16[72,3072]{1,0:T(8,128)(2,1)S(1)} %reshape.130, bf16[3072,4096]{1,0:T(8,128)(2,1)} %param.23), kind=kOutput, calls=%fused_computation.54 | convolution fusion | flops 1811939328 | bytes 26787840 | tf_op jit(solution)/shard_map/dot_general | solution.py:41
  69.6 0.7 copy-done.4
  70.3 0.1 fusion.27
  70.4 2.5 %psum.29 = f32[16,4]{0,1:T(4,128)S(1)} all-reduce(f32[16,4]{0,1:T(4,128)S(1)} %fusion.27), channel_id=1, replica_groups=mesh['group'=2,'node'=8,'tp'=2] {'tp'}, use_global_device_ids=true, to_apply=%region_4.5 | all-reduce | flops 64 | bytes 512 | tf_op jit(solution)/shard_map/psum | solution.py:76
  73.0 0.2 multiply_reduce_fusion.2
  73.2 17.4 %all-reduce.3.cloned.1.call-done = (f32[72,4096]{1,0:T(8,128)}, f32[72,4096]{1,0:T(8,128)}) async-done(((f32[72,4096]{1,0:T(8,128)}, f32[72,4096]{1,0:T(8,128)}), (f32[72,4096]{1,0:T(8,128)}, f32[72,4096]{1,0:T(8,128)})) %all-reduce.3.cloned.1.call-update) | async-done | bytes 2359312 | tf_op jit(solution)/shard_map/psum | solution.py:43
  90.5 13.3 %convolution_convert_fusion = bf16[72,3072]{1,0:T(8,128)(2,1)S(1)} fusion(bf16[4096,3072]{1,0:T(8,128)(2,1)} %param.25, f32[72,4096]{1,0:T(8,128)} %get-tuple-element.5, f32[72,4096]{1,0:T(8,128)} %get-tuple-element.6), kind=kOutput, calls=%fused_computation | convolution fusion | flops 1813929984 | bytes 27967488 | tf_op jit(solution)/shard_map/dot_general | solution.py:45
  103.9 1.1 reshape.131
  104.9 5.8 %all-to-all-start.1 = ((bf16[8,9,3072]{2,1,0:T(8,128)(2,1)}), bf16[8,9,3072]{2,1,0:T(8,128)(2,1)S(1)}, u32[]{:S(2)}, u32[]{:S(2)}) async-start(bf16[8,9,3072]{2,1,0:T(8,128)(2,1)} %reshape.131), calls=%async_computation.1 | async-start | bytes 1572864 | tf_op jit(solution)/shard_map/all_to_all | solution.py:108
  111.1 0.4 fusion.9
  111.5 19.9 %all-to-all-done.1 = bf16[8,9,3072]{2,1,0:T(8,128)(2,1)S(1)} async-done(((bf16[8,9,3072]{2,1,0:T(8,128)(2,1)}), bf16[8,9,3072]{2,1,0:T(8,128)(2,1)S(1)}, u32[]{:S(2)}, u32[]{:S(2)}) %all-to-all-start.1) | async-done | bytes 442400 | tf_op jit(solution)/shard_map/all_to_all | solution.py:108
  131.3 0.1 convert_reduce_fusion
  131.5 1.6 %fusion.1 = bf16[16,3072]{1,0:T(8,128)(2,1)} fusion(f32[4,9,3072]{2,1,0:T(8,128)S(1)} %convert_reduce_fusion, f32[16,3072]{1,0:T(8,128)S(1)} %reshape.128, bf16[16,3072]{1,0:T(8,128)(2,1)S(1)} %copy-done.2, f32[16,4,9]{2,1,0:T(4,128)S(1)} %fusion.9), kind=kOutput, calls=%fused_computation.4 | convolution fusion | flops 21430272 | bytes 837888 | tf_op jit(solution)/shard_map/res,esd->rd/dot_general | solution.py:113
  (30 shorter events, 1.1 us)
Async XLA Ops:
  6.5 8.4 %copy-start = (bf16[16,4,96,128]{3,2,1,0:T(8,128)(2,1)S(1)}, bf16[16,4,96,128]{3,2,1,0:T(8,128)(2,1)}, u32[]{:S(2)}) copy-start(bf16[16,4,96,128]{3,2,1,0:T(8,128)(2,1)} %param.18) | copy-start | bytes 4718596
  6.5 84.0 %all-reduce.3.cloned.1.call-start = ((), (), s32[]{:S(2)}) async-start(), calls=%async_computation.2 | async-start | bytes 4718592 | tf_op jit(solution)/shard_map/psum | solution.py:43
  15.0 0.9 copy-start.2
  15.0 3.6 %copy-start.3 = (f32[3072]{0:T(1024)S(1)}, f32[3072]{0:T(1024)}, u32[]{:S(2)}) copy-start(f32[3072]{0:T(1024)} %param.21) | copy-start | bytes 36868
  69.6 0.7 copy-start.4
  104.9 26.4 %all-to-all-start.1 = ((bf16[8,9,3072]{2,1,0:T(8,128)(2,1)}), bf16[8,9,3072]{2,1,0:T(8,128)(2,1)S(1)}, u32[]{:S(2)}, u32[]{:S(2)}) async-start(bf16[8,9,3072]{2,1,0:T(8,128)(2,1)} %reshape.131), calls=%async_computation.1 | async-start | bytes 1572864 | tf_op jit(solution)/shard_map/all_to_all | solution.py:108
  111.0 22.1 %copy-start.1 = (bf16[16,4,96,128]{3,2,1,0:T(8,128)(2,1)S(1)}, bf16[16,4,96,128]{3,2,1,0:T(8,128)(2,1)}, u32[]{:S(2)}) copy-start(bf16[16,4,96,128]{3,2,1,0:T(8,128)(2,1)} %param.18) | copy-start | bytes 4718596
Sparse Core Ops, SparseCore 0:
  69.7 20.7 all-reduce.2
where the time goes:
time: 140 us
  matrix products  41.9 us (30%)
  waiting for transfers between devices  37.2 us (27%)
  blocking collectives  32.4 us (23%)
  between operations  13.5 us (10%)
  local copies, waits for them, and re-layouts  6.25 us (4%)
  starting transfers between devices  5.78 us (4%)
  other arithmetic  2.81 us (2%)
    all_to_all x1, blocking collectives, local(): lax.all_to_all(outgoing, 'node', split_axis=0, concat_axis=0, tiled=True)  27.4 us
    all_to_all x1, waiting for transfers between devices, local(): lax.all_to_all(computed, 'node', split_axis=0, concat_axis=0, tiled=True)  19.9 us
    psum x1, waiting for transfers between devices, expert_block(): gate_value, up_value = lax.psum((gate_part, up_part), 'tp')  17.4 us
    dot_general x1, matrix products, expert_block(): jnp.dot(hidden, down_weight, preferred_element_type=jnp.float32)  13.3 us
    dot_general x1, matrix products, expert_block(): up_part = jnp.dot(flattened, up_weight, preferred_element_type=jnp.float32)  11.5 us
    dot_general x1, matrix products, expert_block(): jnp.dot(flattened, gate_weight, preferred_element_type=jnp.float32)  11.5 us
    all_to_all x1, starting transfers between devices, local(): lax.all_to_all(computed, 'node', split_axis=0, concat_axis=0, tiled=True)  5.78 us
  transfers between devices with their start and end apart: 2, of which 2 were waited for; matrix products, arithmetic and copies ran while one was open for 1% of the time, Pallas kernels for 0%

commit v1 on v0

v1 whole, which is shorter than its diff:
```python
import functools
import math

import jax
import jax.numpy as jnp
from jax import lax
from jax.experimental import pallas as pl
from jax.experimental.pallas import tpu as pltpu
from jax.sharding import PartitionSpec as P

F32, BF16 = jnp.float32, jnp.bfloat16
NT = (((1,), (1,)), ((), ()))
SLOT_MAX = 48
CW = 512


def layer_kernel(
    cfg,
    lens_ref,
    routes_ref,
    res_ref,
    q_ref,
    nk_ref,
    nv_ref,
    ck_hbm,
    cv_hbm,
    gain_ref,
    router_ref,
    gate_hbm,
    up_hbm,
    down_hbm,
    out_ref,
    kbuf,
    vbuf,
    wbuf,
    xbuf,
    mixed,
    stat_s,
    stat_r,
    own_part,
    psend,
    precv,
    hidden,
    xsend,
    xrecv,
    xown,
    zsend,
    zrecv,
    zown,
    cache_sem,
    wsem,
    stat_sem,
    dsend_sem,
    drecv_sem,
    psend_sem,
    precv_sem,
    xsend_sem,
    xrecv_sem,
    zsend_sem,
    zrecv_sem,
):
    A, B, R, W, FF, KV, L, H = cfg
    N, M = A * B, A * B * R
    HQ = W // (KV * H)
    KB = min(1024, FF)
    nc, nk = FF // CW, W // 1024
    nj, nd = W // CW, FF // KB
    direct = nc * nk * 2 + nj * nd <= SLOT_MAX
    node = lax.axis_index("node")
    tp = lax.axis_index("tp")
    a_me, b_me = lax.div(node, B), lax.rem(node, B)
    mine = b_me * A + a_me

    def outer(i):
        return lax.rem(a_me + i, A)

    def inner(i):
        return lax.rem(b_me + i, B)

    def dev(a, b):
        return {"node": a * B + b}

    def gu_copy(c, w, k):
        slot = (c * 2 + w) * nk + k
        src = gate_hbm if w == 0 else up_hbm
        col = pl.multiple_of(c * CW, CW)
        return pltpu.make_async_copy(
            src.at[pl.ds(k * 1024, 1024), pl.ds(col, CW)], wbuf.at[slot], wsem.at[slot]
        )

    def down_slot(j, k):
        return j * nd + k + (nc * nk * 2 if direct else 0)

    def down_copy(j, k):
        slot = down_slot(j, k)
        col = pl.multiple_of(j * CW, CW)
        return pltpu.make_async_copy(
            down_hbm.at[pl.ds(k * KB, KB), pl.ds(col, CW)],
            wbuf.at[slot, pl.ds(0, KB)],
            wsem.at[slot],
        )

    kcopy = pltpu.make_async_copy(ck_hbm, kbuf, cache_sem.at[0])
    vcopy = pltpu.make_async_copy(cv_hbm, vbuf, cache_sem.at[1])
    kcopy.start()
    vcopy.start()

    @pl.loop(0, nc)
    def _(c):
        for w in range(2):
            for k in range(nk):
                gu_copy(c, w, k).start()

    if direct:

        @pl.loop(0, nj)
        def _(j):
            for k in range(nd):
                down_copy(j, k).start()

    barrier = pltpu.get_barrier_semaphore()
    pl.semaphore_signal(
        barrier, inc=1, device_id={"tp": 1 - tp}, device_id_type=pl.DeviceIdType.MESH
    )
    for i in range(1, A):
        pl.semaphore_signal(
            barrier, inc=1, device_id=dev(outer(i), b_me), device_id_type=pl.DeviceIdType.MESH
        )
    for i in range(1, B):
        pl.semaphore_signal(
            barrier, inc=1, device_id=dev(a_me, inner(i)), device_id_type=pl.DeviceIdType.MESH
        )

    kcopy.wait()
    vcopy.wait()
    factor = 1.0 / math.sqrt(H)
    row128 = lax.broadcasted_iota(jnp.int32, (R, 128), 0)
    lenv = jnp.zeros((R, 128), jnp.int32)
    r0 = jnp.zeros((R, 128), jnp.int32)
    r1 = jnp.zeros((R, 128), jnp.int32)
    for r in range(R):
        lenv = jnp.where(row128 == r, lens_ref[r], lenv)
        r0 = jnp.where(row128 == r, routes_ref[0, r], r0)
        r1 = jnp.where(row128 == r, routes_ref[1, r], r1)
    col = lax.broadcasted_iota(jnp.int32, (R, R * L), 1)
    row = lax.broadcasted_iota(jnp.int32, (R, R * L), 0)
    valid = jnp.logical_and(col >= row * L, col < row * L + lenv[:, 0:1])
    bias = jnp.where(valid, 0.0, -jnp.inf).astype(F32)
    bias = jnp.concatenate([bias] * HQ, axis=0)
    square = jnp.zeros((R, 1), F32)
    logits = jnp.zeros((R, router_ref.shape[0]), F32)
    for g in range(KV):
        base = g * HQ * H
        q = jnp.concatenate([q_ref[:, base + h * H : base + (h + 1) * H] for h in range(HQ)], axis=0)
        keys = kbuf[:, g].reshape(R * L, H)
        values = vbuf[:, g].reshape(R * L, H)
        scores = lax.dot_general(q, keys, NT, preferred_element_type=F32) * factor + bias
        own_key = jnp.concatenate([nk_ref[:, g * H : (g + 1) * H].astype(F32)] * HQ, axis=0)
        own = jnp.sum(q.astype(F32) * own_key, axis=1, keepdims=True) * factor
        highest = jnp.maximum(jnp.max(scores, axis=1, keepdims=True), own)
        weights = jnp.exp(scores - highest)
        own_weight = jnp.exp(own - highest)
        total = jnp.sum(weights, axis=1, keepdims=True) + own_weight
        probs = (weights / total).astype(BF16)
        own_prob = (own_weight / total).astype(BF16).astype(F32)
        attended = jnp.dot(probs, values, preferred_element_type=F32)
        own_value = jnp.concatenate([nv_ref[:, g * H : (g + 1) * H].astype(F32)] * HQ, axis=0)
        attended = attended + own_prob * own_value
        for h in range(HQ):
            lo = base + h * H
            m = res_ref[:, lo : lo + H].astype(F32) + attended[h * R : (h + 1) * R]
            mixed[:, lo : lo + H] = m
            square = square + jnp.sum(m * m, axis=1, keepdims=True)
    gained = (mixed[...] * gain_ref[...]).astype(BF16)
    logits = lax.dot_general(gained, router_ref[...], NT, preferred_element_type=F32)
    stat_s[...] = jnp.zeros_like(stat_s)
    stat_s[:, 0:A] = logits
    stat_s[:, A : A + 1] = square

    pl.semaphore_wait(barrier, 1 + (A - 1) + (B - 1))
    stat_copy = pltpu.make_async_remote_copy(
        stat_s,
        stat_r,
        stat_sem.at[0],
        stat_sem.at[1],
        device_id={"tp": 1 - tp},
        device_id_type=pl.DeviceIdType.MESH,
    )
    stat_copy.start()
    stat_copy.wait()
    stat = stat_s[...] + stat_r[...]
    inverse = lax.rsqrt(stat[:, A : A + 1] / (2 * W) + 1e-05)
    logit = stat * inverse
    lane = lax.broadcasted_iota(jnp.int32, (R, 128), 1)
    p0 = jnp.sum(jnp.where(lane == r0, logit, 0.0), axis=1, keepdims=True)
    p1 = jnp.sum(jnp.where(lane == r1, logit, 0.0), axis=1, keepdims=True)
    w0 = 1.0 / (1.0 + jnp.exp(p1 - p0))
    w1 = 1.0 / (1.0 + jnp.exp(p0 - p1))
    pair = jnp.where(lane == r0, w0, 0.0) + jnp.where(lane == r1, w1, 0.0)
    pair_hi = pair.astype(BF16)
    lane_lo = lane - A
    low = jnp.where(lane_lo == r0, w0, 0.0) + jnp.where(lane_lo == r1, w1, 0.0)
    low = (low - low.astype(BF16).astype(F32)).astype(BF16)
    xbuf[mine, :, W : W + 128] = pair_hi + low
    xbuf[mine, :, 0:W] = (mixed[...] * inverse * gain_ref[...]).astype(BF16)

    def x_copy(block, sem, a, b):
        return pltpu.make_async_remote_copy(
            xbuf.at[block],
            xbuf.at[block],
            dsend_sem.at[sem],
            drecv_sem.at[block],
            device_id=dev(a, b),
            device_id_type=pl.DeviceIdType.MESH,
        )

    def z_send(i):
        return x_copy(mine, b_me * A + outer(i), outer(i), b_me)

    def relay(i, t):
        return x_copy(b_me * A + outer(i), inner(t) * A + outer(i), a_me, inner(t))

    def arrival(i, t):
        return x_copy(inner(t) * A + outer(i), 0, a_me, inner(1))

    for i in range(1, A):
        z_send(i).start()
    for t in range(1, B):
        relay(0, t).start()
    for i in range(1, A):
        arrival(i, 0).wait_recv()
        for t in range(1, B):
            relay(i, t).start()
    for t in range(1, B):
        for i in range(A):
            arrival(i, t).wait_recv()

    def part_copy(c):
        s = lax.rem(c, 2)
        return pltpu.make_async_remote_copy(
            psend.at[s],
            precv.at[c],
            psend_sem.at[s],
            precv_sem.at[c],
            device_id={"tp": 1 - tp},
            device_id_type=pl.DeviceIdType.MESH,
        )

    def finish(c):
        s = lax.rem(c, 2)
        part_copy(c).wait_recv()
        gate = own_part[s, 0] + precv[c, 0].astype(F32)
        up = own_part[s, 1] + precv[c, 1].astype(F32)
        value = (gate / (1.0 + jnp.exp(-gate)) * up).astype(BF16)
        hidden[:, pl.ds(pl.multiple_of(c * CW, CW), CW)] = value

    @pl.loop(0, nc)
    def _(c):
        s = lax.rem(c, 2)

        @pl.when(c >= 2)
        def _():
            part_copy(c - 2).wait_send()

        for w in range(2):
            acc = None
            for k in range(nk):
                gu_copy(c, w, k).wait()
                lhs = xbuf[:, :, k * 1024 : (k + 1) * 1024].reshape(M, 1024)
                term = jnp.dot(lhs, wbuf[(c * 2 + w) * nk + k], preferred_element_type=F32)
                acc = term if acc is None else acc + term
            own_part[s, w] = acc
            psend[s, w] = acc.astype(BF16)
        part_copy(c).start()
        if not direct:
            per = 2 * nk // nd if (2 * nk) % nd == 0 else 1

            @pl.when(c * per < nj)
            def _():
                for p in range(per):

                    @pl.when(c * per + p < nj)
                    def _():
                        for k in range(nd):
                            down_copy(c * per + p, k).start()

        @pl.when(c >= 1)
        def _():
            finish(c - 1)

    finish(nc - 1)
    for c in range(max(0, nc - 2), nc):
        part_copy(c).wait_send()

    side = xbuf[:, :, W : W + 128].reshape(M, 128).astype(F32)
    lane_m = lax.broadcasted_iota(jnp.int32, (M, 128), 1)
    keep = jnp.logical_or(lane_m == a_me, lane_m == a_me + A)
    pairw = jnp.sum(jnp.where(keep, side, 0.0), axis=1, keepdims=True)

    G = A * R

    def xs_copy(j, t):
        other = inner(t)
        return pltpu.make_async_remote_copy(
            xsend.at[j, other],
            xrecv.at[j, b_me],
            xsend_sem.at[j, other],
            xrecv_sem.at[j, b_me],
            device_id=dev(a_me, other),
            device_id_type=pl.DeviceIdType.MESH,
        )

    def xs_arrival(j, t):
        other = inner(t)
        return pltpu.make_async_remote_copy(
            xsend.at[j, b_me],
            xrecv.at[j, other],
            xsend_sem.at[j, b_me],
            xrecv_sem.at[j, other],
            device_id=dev(a_me, other),
            device_id_type=pl.DeviceIdType.MESH,
        )

    def zs_copy(j, i):
        other = outer(i)
        return pltpu.make_async_remote_copy(
            zsend.at[j, other],
            zrecv.at[j, a_me],
            zsend_sem.at[j, other],
            zrecv_sem.at[j, a_me],
            device_id=dev(other, b_me),
            device_id_type=pl.DeviceIdType.MESH,
        )

    def zs_arrival(j, i):
        other = outer(i)
        return pltpu.make_async_remote_copy(
            zsend.at[j, a_me],
            zrecv.at[j, other],
            zsend_sem.at[j, a_me],
            zrecv_sem.at[j, other],
            device_id=dev(other, b_me),
            device_id_type=pl.DeviceIdType.MESH,
        )

    def stage_one(j):
        acc = None
        for k in range(nd):
            down_copy(j, k).wait()
            term = jnp.dot(
                hidden[:, k * KB : (k + 1) * KB],
                wbuf[down_slot(j, k), 0:KB],
                preferred_element_type=F32,
            )
            acc = term if acc is None else acc + term
        acc = acc * pairw
        for b in range(B):
            xsend[j, b] = acc[b * G : (b + 1) * G].astype(BF16)
            mask = jnp.where(b_me == b, 1.0, 0.0)
            if b == 0:
                kept = acc[0:G] * mask
            else:
                kept = kept + acc[b * G : (b + 1) * G] * mask
        xown[lax.rem(j, 2)] = kept
        for t in range(1, B):
            xs_copy(j, t).start()

    def stage_two(j):
        total = xown[lax.rem(j, 2)]
        for t in range(1, B):
            xs_arrival(j, t).wait_recv()
            total = total + xrecv[j, inner(t)].astype(F32)
        zown[j] = total
        for a in range(A):
            zsend[j, a] = total[a * R : (a + 1) * R].astype(BF16)
        for i in range(1, A):
            zs_copy(j, i).start()

    def stage_three(j):
        cols = pl.ds(pl.multiple_of(j * CW, CW), CW)
        total = mixed[:, cols] + zown[j, pl.ds(pl.multiple_of(a_me * R, R), R), :]
        for i in range(1, A):
            zs_arrival(j, i).wait_recv()
            total = total + zrecv[j, outer(i)].astype(F32)
        out_ref[:, cols] = total.astype(BF16)

    @pl.loop(0, nj)
    def _(j):
        stage_one(j)

        @pl.when(j >= 1)
        def _():
            stage_two(j - 1)

        @pl.when(j >= 2)
        def _():
            stage_three(j - 2)

    stage_two(nj - 1)
    stage_three(nj - 2)
    stage_three(nj - 1)

    for i in range(1, A):
        z_send(i).wait_send()
    for t in range(1, B):
        for i in range(A):
            relay(i, t).wait_send()

    @pl.loop(0, nj)
    def _(j):
        for t in range(1, B):
            xs_copy(j, t).wait_send()
        for i in range(1, A):
            zs_copy(j, i).wait_send()


def local(
    residual,
    queries,
    new_keys,
    new_values,
    cache_keys,
    cache_values,
    lengths,
    routes,
    norm_gain,
    router_weight,
    gate_weight,
    up_weight,
    down_weight,
):
    R, W = residual.shape
    FF = gate_weight.shape[1]
    _, KV, L, H = cache_keys.shape
    A = router_weight.shape[1]
    B = lax.axis_size("node") // A
    N, M = A * B, A * B * R
    KB = min(1024, FF)
    nc, nk, nj, nd = FF // CW, W // 1024, W // CW, FF // KB
    gu = nc * nk * 2
    slots = gu + nj * nd if gu + nj * nd <= SLOT_MAX else gu
    cfg = (A, B, R, W, FF, KV, L, H)
    vmem = pl.BlockSpec(memory_space=pltpu.VMEM)
    smem = pl.BlockSpec(memory_space=pltpu.SMEM)
    hbm = pl.BlockSpec(memory_space=pl.ANY)
    dma = pltpu.SemaphoreType.DMA
    return pl.pallas_call(
        functools.partial(layer_kernel, cfg),
        out_shape=jax.ShapeDtypeStruct((R, W), BF16),
        in_specs=[smem, smem, vmem, vmem, vmem, vmem, hbm, hbm, vmem, vmem, hbm, hbm, hbm],
        out_specs=vmem,
        scratch_shapes=[
            pltpu.VMEM((R, KV, L, H), BF16),
            pltpu.VMEM((R, KV, L, H), BF16),
            pltpu.VMEM((slots, 1024, CW), BF16),
            pltpu.VMEM((N, R, W + 128), BF16),
            pltpu.VMEM((R, W), F32),
            pltpu.VMEM((R, 128), F32),
            pltpu.VMEM((R, 128), F32),
            pltpu.VMEM((2, 2, M, CW), F32),
            pltpu.VMEM((2, 2, M, CW), BF16),
            pltpu.VMEM((nc, 2, M, CW), BF16),
            pltpu.VMEM((M, FF), BF16),
            pltpu.VMEM((nj, B, A * R, CW), BF16),
            pltpu.VMEM((nj, B, A * R, CW), BF16),
            pltpu.VMEM((2, A * R, CW), F32),
            pltpu.VMEM((nj, A, R, CW), BF16),
            pltpu.VMEM((nj, A, R, CW), BF16),
            pltpu.VMEM((nj, A * R, CW), F32),
            dma((2,)),
            dma((slots,)),
            dma((2,)),
            dma((N,)),
            dma((N,)),
            dma((2,)),
            dma((nc,)),
            dma((nj, B)),
            dma((nj, B)),
            dma((nj, A)),
            dma((nj, A)),
        ],
        compiler_params=pltpu.CompilerParams(
            collective_id=0, has_side_effects=True, vmem_limit_bytes=63 * 1024 * 1024
        ),
    )(
        lengths,
        routes.T,
        residual,
        queries,
        new_keys,
        new_values,
        cache_keys,
        cache_values,
        norm_gain.reshape(1, -1),
        router_weight.T,
        gate_weight,
        up_weight,
        down_weight,
    )


def solution(mesh):
    placed = (
        P(("group", "node"), "tp"),
        P(("group", "node"), "tp"),
        P(("group", "node"), "tp"),
        P(("group", "node"), "tp"),
        P(("group", "node"), "tp", None, None),
        P(("group", "node"), "tp", None, None),
        P(("group", "node")),
        P(("group", "node"), None),
        P("tp"),
        P("tp", None),
        P("tp", "node"),
        P("tp", "node"),
        P("node", "tp"),
    )
    return jax.shard_map(
        local, mesh=mesh, in_specs=placed, out_specs=P(("group", "node"), "tp"), check_vma=False
    )
```

time: 140 us -> 66.8 us (0.48)
  Pallas kernels: 0 us -> 65.1 us
  matrix products: 41.9 us -> 0 us
  waiting for transfers between devices: 37.2 us -> 0 us
  blocking collectives: 32.4 us -> 0 us
  between operations: 13.5 us -> 0.01 us
  starting transfers between devices: 5.78 us -> 0 us
  local copies, waits for them, and re-layouts: 6.25 us -> 1.54 us
  other arithmetic: 2.81 us -> 0 us
    pallas_call x0 -> x1, Pallas kernels: none -> 65.1 us  [local(): pl.pallas_call(functools.partial(layer_kernel, cfg), out_shape=jax.ShapeD...]
    dot_general x10 -> x0, matrix products: 41.9 us -> none  [the longest x1 13.3 us: expert_block(): jnp.dot(hidden, down_weight, preferred_element_type=jnp.float32)]
    all_to_all x1 -> x0, blocking collectives: 27.4 us -> none  [local(): lax.all_to_all(outgoing, 'node', split_axis=0, concat_axis=0, tiled=True)]
    all_to_all x1 -> x0, waiting for transfers between devices: 19.9 us -> none  [local(): lax.all_to_all(computed, 'node', split_axis=0, concat_axis=0, tiled=True)]
    psum x1 -> x0, waiting for transfers between devices: 17.4 us -> none  [expert_block(): gate_value, up_value = lax.psum((gate_part, up_part), 'tp')]
    all_to_all x1 -> x0, starting transfers between devices: 5.78 us -> none  [local(): lax.all_to_all(computed, 'node', split_axis=0, concat_axis=0, tiled=True)]
    psum x2 -> x0, blocking collectives: 5.04 us -> none  [the longest x1 2.58 us: local(): square_sum = lax.psum(jnp.sum(mixed_in * mixed_in, axis=1), 'tp')]
    reshape x5 -> x0, local copies, waits for them, and re-layouts: 3.08 us -> none  [the longest x1 1.07 us: expert_block(): return produced.reshape(sources, slot_part, -1)]
  transfers between devices with their start and end apart: 2 -> 0, of which waited for: 2 -> 0; matrix products, arithmetic and copies ran while one was open for 1% -> 0% of each run, Pallas kernels for 0% -> 0%
where the time goes in v1:
time: 66.8 us; the launch traced here: 66.6 us
  Pallas kernels  65.1 us (97%)
  local copies, waits for them, and re-layouts  1.54 us (2%)
    pallas_call x1, Pallas kernels, local(): pl.pallas_call(functools.partial(layer_kernel, cfg), out_shape=jax.ShapeD...  65.1 us
    unnamed x1, local copies, waits for them, and re-layouts  1.54 us

profile of v1, /device:TPU:0, one launch (start us, length us, event | category | flops | bytes accessed | tf_op | source)
XLA Modules:
  0.0 66.6 jit_solution(2122081372030008903)
XLA Ops:
  0.0 65.1 %shard_map.127 = bf16[16,3072]{1,0:T(8,128)(2,1)} custom-call(s32[16]{0:T(128)} %lens_ref.1, s32[2,16]{1,0:T(2,128)} %bitcast.5, bf16[16,3072]{1,0:T(8,128)(2,1)} %res_ref.1, bf16[16,3072]{1,0:T(8,128)(2,1)} %q_ref.1, bf16[16,512]{1,0:T(8,128)(2,1)} %nk_ref.1, bf16[16,512]{1,0:T(8,128)(2,1)} %nv_ref.1, bf16[16,4,96,128]{3,2,1,0:T(8,128)(2,1)} %ck_hbm.1, ...), custom_call_target="tpu_custom_call" | custom-call | tf_op jit(solution)/shard_map/pallas_call | solution.py:447
  65.1 1.5 %copy.15 = bf16[16,3072]{1,0:T(8,128)(2,1)} copy(bf16[16,3072]{1,0:T(8,128)(2,1)} %shard_map.127) | data formatting | bytes 196608

commit v2 on v1

--- a/solution.py
+++ b/solution.py
@@ -34,6 +34,7 @@
     vbuf,
     wbuf,
     xbuf,
+    side_buf,
     mixed,
     stat_s,
     stat_r,
@@ -51,6 +52,7 @@
     wsem,
     stat_sem,
     dsend_sem,
+    rsend_sem,
     drecv_sem,
     psend_sem,
     precv_sem,
@@ -201,39 +203,87 @@
     lane_lo = lane - A
     low = jnp.where(lane_lo == r0, w0, 0.0) + jnp.where(lane_lo == r1, w1, 0.0)
     low = (low - low.astype(BF16).astype(F32)).astype(BF16)
-    xbuf[mine, :, W : W + 128] = pair_hi + low
-    xbuf[mine, :, 0:W] = (mixed[...] * inverse * gain_ref[...]).astype(BF16)
-
-    def x_copy(block, sem, a, b):
+    side_buf[mine] = pair_hi + low
+    normed = (mixed[...] * inverse * gain_ref[...]).astype(BF16)
+    for k in range(nk):
+        xbuf[k, mine] = normed[:, k * 1024 : (k + 1) * 1024]
+
+    def x_copy(k, block, sem, a, b):
+        ref = side_buf.at[block] if k == nk else xbuf.at[k, block]
         return pltpu.make_async_remote_copy(
-            xbuf.at[block],
-            xbuf.at[block],
-            dsend_sem.at[sem],
-            drecv_sem.at[block],
+            ref,
+            ref,
+            sem,
+            drecv_sem.at[k, block],
             device_id=dev(a, b),
             device_id_type=pl.DeviceIdType.MESH,
         )
 
-    def z_send(i):
-        return x_copy(mine, b_me * A + outer(i), outer(i), b_me)
-
-    def relay(i, t):
-        return x_copy(b_me * A + outer(i), inner(t) * A + outer(i), a_me, inner(t))
-
-    def arrival(i, t):
-        return x_copy(inner(t) * A + outer(i), 0, a_me, inner(1))
-
-    for i in range(1, A):
-        z_send(i).start()
-    for t in range(1, B):
-        relay(0, t).start()
-    for i in range(1, A):
-        arrival(i, 0).wait_recv()
+    def pass_up(k, a):
+        return x_copy(k, b_me * A + a, dsend_sem.at[k, 0, a], a_me + 1, b_me)
+
+    def pass_down(k, a):
+        return x_copy(k, b_me * A + a, dsend_sem.at[k, 1, a], a_me - 1, b_me)
+
+    def relay(k, a, t):
+        sem = rsend_sem.at[k, inner(t) * A + a]
+        return x_copy(k, b_me * A + a, sem, a_me, inner(t))
+
+    def arrival(k, a, t):
+        return x_copy(k, inner(t) * A + a, dsend_sem.at[0, 0, 0], a_me, inner(1))
+
+    def below_above(h):
+        low_in = jnp.logical_and(a_me >= h, a_me < A - 1)
+        high_in = jnp.logical_and(a_me + h < A, a_me > 0)
+        return low_in, high_in
+
+    parts = [nk] + list(range(nk))
+    for k in parts:
+
+        @pl.when(a_me < A - 1)
+        def _():
+            pass_up(k, a_me).start()
+
+        @pl.when(a_me > 0)
+        def _():
+            pass_down(k, a_me).start()
+
         for t in range(1, B):
-            relay(i, t).start()
-    for t in range(1, B):
-        for i in range(A):
-            arrival(i, t).wait_recv()
+            relay(k, a_me, t).start()
+    for h in range(1, A):
+        low_in, high_in = below_above(h)
+        for k in parts:
+
+            @pl.when(a_me >= h)
+            def _():
+                arrival(k, a_me - h, 0).wait_recv()
+
+            @pl.when(low_in)
+            def _():
+                pass_up(k, a_me - h).start()
+
+            @pl.when(a_me + h < A)
+            def _():
+                arrival(k, a_me + h, 0).wait_recv()
+
+            @pl.when(high_in)
+            def _():
+                pass_down(k, a_me + h).start()
+
+            for t in range(1, B):
+
+                @pl.when(a_me >= h)
+                def _():
+                    relay(k, a_me - h, t).start()
+
+                @pl.when(a_me + h < A)
+                def _():
+                    relay(k, a_me + h, t).start()
+
+    for k in parts:
+        for t in range(1, B):
+            for i in range(A):
+                arrival(k, outer(i), t).wait_recv()
 
     def part_copy(c):
         s = lax.rem(c, 2)
@@ -266,7 +316,7 @@
             acc = None
             for k in range(nk):
                 gu_copy(c, w, k).wait()
-                lhs = xbuf[:, :, k * 1024 : (k + 1) * 1024].reshape(M, 1024)
+                lhs = xbuf[k].reshape(M, 1024)
                 term = jnp.dot(lhs, wbuf[(c * 2 + w) * nk + k], preferred_element_type=F32)
                 acc = term if acc is None else acc + term
             own_part[s, w] = acc
@@ -292,7 +342,7 @@
     for c in range(max(0, nc - 2), nc):
         part_copy(c).wait_send()
 
-    side = xbuf[:, :, W : W + 128].reshape(M, 128).astype(F32)
+    side = side_buf[...].reshape(M, 128).astype(F32)
     lane_m = lax.broadcasted_iota(jnp.int32, (M, 128), 1)
     keep = jnp.logical_or(lane_m == a_me, lane_m == a_me + A)
     pairw = jnp.sum(jnp.where(keep, side, 0.0), axis=1, keepdims=True)
@@ -400,11 +450,21 @@
     stage_three(nj - 2)
     stage_three(nj - 1)
 
-    for i in range(1, A):
-        z_send(i).wait_send()
-    for t in range(1, B):
-        for i in range(A):
-            relay(i, t).wait_send()
+    for k in parts:
+        for h in range(A):
+            low_in, high_in = below_above(h)
+
+            @pl.when(low_in)
+            def _():
+                pass_up(k, a_me - h).wait_send()
+
+            @pl.when(high_in)
+            def _():
+                pass_down(k, a_me + h).wait_send()
+
+        for t in range(1, B):
+            for i in range(A):
+                relay(k, outer(i), t).wait_send()
 
     @pl.loop(0, nj)
     def _(j):
@@ -453,7 +513,8 @@
             pltpu.VMEM((R, KV, L, H), BF16),
             pltpu.VMEM((R, KV, L, H), BF16),
             pltpu.VMEM((slots, 1024, CW), BF16),
-            pltpu.VMEM((N, R, W + 128), BF16),
+            pltpu.VMEM((nk, N, R, 1024), BF16),
+            pltpu.VMEM((N, R, 128), BF16),
             pltpu.VMEM((R, W), F32),
             pltpu.VMEM((R, 128), F32),
             pltpu.VMEM((R, 128), F32),
@@ -470,8 +531,9 @@
             dma((2,)),
             dma((slots,)),
             dma((2,)),
-            dma((N,)),
-            dma((N,)),
+            dma((nk + 1, 2, A)),
+            dma((nk + 1, N)),
+            dma((nk + 1, N)),
             dma((2,)),
             dma((nc,)),
             dma((nj, B)),

time: 66.8 us -> 62.6 us (0.937)
  Pallas kernels: 65.1 us -> 60.9 us
    pallas_call x1, Pallas kernels: 65.1 us -> 60.9 us  [local(): pl.pallas_call(functools.partial(layer_kernel, cfg), out_shape=jax.ShapeD...]
where the time goes in v2:
time: 62.6 us; the launch traced here: 62.4 us
  Pallas kernels  60.9 us (97%)
  local copies, waits for them, and re-layouts  1.54 us (2%)
    pallas_call x1, Pallas kernels, local(): pl.pallas_call(functools.partial(layer_kernel, cfg), out_shape=jax.ShapeD...  60.9 us
    unnamed x1, local copies, waits for them, and re-layouts  1.54 us

profile of v2, /device:TPU:0, one launch (start us, length us, event | category | flops | bytes accessed | tf_op | source)
XLA Modules:
  0.0 62.4 jit_solution(8800464687525168254)
XLA Ops:
  0.0 60.9 %shard_map.127 = bf16[16,3072]{1,0:T(8,128)(2,1)} custom-call(s32[16]{0:T(128)} %lens_ref.1, s32[2,16]{1,0:T(2,128)} %bitcast.5, bf16[16,3072]{1,0:T(8,128)(2,1)} %res_ref.1, bf16[16,3072]{1,0:T(8,128)(2,1)} %q_ref.1, bf16[16,512]{1,0:T(8,128)(2,1)} %nk_ref.1, bf16[16,512]{1,0:T(8,128)(2,1)} %nv_ref.1, bf16[16,4,96,128]{3,2,1,0:T(8,128)(2,1)} %ck_hbm.1, ...), custom_call_target="tpu_custom_call" | custom-call | tf_op jit(solution)/shard_map/pallas_call | solution.py:507
  60.9 1.5 %copy.15 = bf16[16,3072]{1,0:T(8,128)(2,1)} copy(bf16[16,3072]{1,0:T(8,128)(2,1)} %shard_map.127) | data formatting | bytes 196608

commit v3 on v2

--- a/solution.py
+++ b/solution.py
@@ -411,12 +411,12 @@
                 kept = acc[0:G] * mask
             else:
                 kept = kept + acc[b * G : (b + 1) * G] * mask
-        xown[lax.rem(j, 2)] = kept
+        xown[lax.rem(j, 3)] = kept
         for t in range(1, B):
             xs_copy(j, t).start()
 
     def stage_two(j):
-        total = xown[lax.rem(j, 2)]
+        total = xown[lax.rem(j, 3)]
         for t in range(1, B):
             xs_arrival(j, t).wait_recv()
             total = total + xrecv[j, inner(t)].astype(F32)
@@ -438,17 +438,16 @@
     def _(j):
         stage_one(j)
 
-        @pl.when(j >= 1)
-        def _():
-            stage_two(j - 1)
-
         @pl.when(j >= 2)
         def _():
-            stage_three(j - 2)
-
+            stage_two(j - 2)
+
+    stage_two(nj - 2)
     stage_two(nj - 1)
-    stage_three(nj - 2)
-    stage_three(nj - 1)
+
+    @pl.loop(0, nj)
+    def _(j):
+        stage_three(j)
 
     for k in parts:
         for h in range(A):
@@ -524,7 +523,7 @@
             pltpu.VMEM((M, FF), BF16),
             pltpu.VMEM((nj, B, A * R, CW), BF16),
             pltpu.VMEM((nj, B, A * R, CW), BF16),
-            pltpu.VMEM((2, A * R, CW), F32),
+            pltpu.VMEM((3, A * R, CW), F32),
             pltpu.VMEM((nj, A, R, CW), BF16),
             pltpu.VMEM((nj, A, R, CW), BF16),
             pltpu.VMEM((nj, A * R, CW), F32),

time: 62.6 us -> 56 us (0.89)
  Pallas kernels: 60.9 us -> 54.3 us
    pallas_call x1, Pallas kernels: 60.9 us -> 54.3 us  [local(): pl.pallas_call(functools.partial(layer_kernel, cfg), out_shape=jax.ShapeD...]
where the time goes in v3:
time: 56 us; the launch traced here: 55.8 us
  Pallas kernels  54.3 us (97%)
  local copies, waits for them, and re-layouts  1.54 us (3%)
    pallas_call x1, Pallas kernels, local(): pl.pallas_call(functools.partial(layer_kernel, cfg), out_shape=jax.ShapeD...  54.3 us
    unnamed x1, local copies, waits for them, and re-layouts  1.54 us

profile of v3, /device:TPU:0, one launch (start us, length us, event | category | flops | bytes accessed | tf_op | source)
XLA Modules:
  0.0 55.8 jit_solution(12418274890729706016)
XLA Ops:
  0.0 54.3 %shard_map.127 = bf16[16,3072]{1,0:T(8,128)(2,1)} custom-call(s32[16]{0:T(128)} %lens_ref.1, s32[2,16]{1,0:T(2,128)} %bitcast.5, bf16[16,3072]{1,0:T(8,128)(2,1)} %res_ref.1, bf16[16,3072]{1,0:T(8,128)(2,1)} %q_ref.1, bf16[16,512]{1,0:T(8,128)(2,1)} %nk_ref.1, bf16[16,512]{1,0:T(8,128)(2,1)} %nv_ref.1, bf16[16,4,96,128]{3,2,1,0:T(8,128)(2,1)} %ck_hbm.1, ...), custom_call_target="tpu_custom_call" | custom-call | tf_op jit(solution)/shard_map/pallas_call | solution.py:506
  54.3 1.5 %copy.15 = bf16[16,3072]{1,0:T(8,128)(2,1)} copy(bf16[16,3072]{1,0:T(8,128)(2,1)} %shard_map.127) | data formatting | bytes 196608
